TPU v7x, 32 devices: a whole 2x2x4 slice. The times are simulated.
32 devices in a mesh: tile: 4 (over y, x), depth: 8 (over z, core).
Axes of the slice: x: 2, y: 2, z: 4, core: 2. Of those that a mesh axis runs over, the one named last changes fastest.
Arguments:
- volume: bfloat16 [4, 8, 128, 128, 128], P('tile', 'depth'), may hold values from -8 to 8
- shear: float32 [4, 8, 2], P('tile', 'depth'), may hold values from -0.5 to 0.5
- absorb: float32 [4, 8], P('tile', 'depth'), may hold values from 0.000390625 to 0.0078125
- color_slope: float32 [3], replicated, may hold values from -3 to 3
- color_bias: float32 [3], replicated, may hold values from -1.5 to 1.5
- frag_tile: int32 [4, 8, 16, 1], P('tile', 'depth'), may hold values from 0 to 3; in each aligned block of 16 rows (0 to 15, 16 to 31, ..., all dimensions but the last counted through in order) at most 4 rows name the same one
- slot_perm: int32 [4, 8, 4, 16], P('tile', 'depth'), may hold values from 0 to 15, each once within a row
- frag_rows: int32 [4, 8, 16], P('tile', 'depth'), may hold values from 1 to 64
- tile_view: int32 [4], replicated, may hold values from 0 to 1
- tile_owner: int32 [4], replicated, may hold values from 0 to 3, each once
Outputs:
- frame: bfloat16 [4, 4, 256, 256], P('tile')
Inputs may be any that keep to these rules, and one draw needn't show every extreme that they name: `frag_tile`: each brick puts at most 4 fragments on one screen tile, and some brick puts exactly 4 there in every draw. `slot_perm`: each row is a permutation of the positions. `tile_owner`: A permutation of the tiles.
All inputs are finite; a program needn't handle non-finite values.
Results may differ from a plain program's by a relative error of at most 0.0035.
Values may be sent and summed in bfloat16 or wider, within the bound.
A program may use at most 64 MiB of HBM per device.

v0:
```python
import functools
import jax
import jax.numpy as jnp
from jax import lax
from jax.experimental import pallas as pl
from jax.experimental.pallas import tpu as pltpu
from jax.sharding import PartitionSpec as P

SAMPLES = 128
RAYS = 256
FRAG = 64
TILE_SIDE = 256
CAP = 4
POS = 16
GROUP = 4
ROWS = 16
TAPS = 4
LOG2E = 1.4426950408889634


def spline(offset):
    size_abs = jnp.abs(offset)
    inner = 2.0 / 3.0 - size_abs * size_abs + 0.5 * size_abs * size_abs * size_abs
    remain = 2.0 - size_abs
    outer = remain * remain * remain / 6.0
    return jnp.where(size_abs < 1.0, inner, jnp.where(size_abs < 2.0, outer, 0.0))


def taps_of(shear_one, side):
    per = RAYS // side
    centred = jnp.arange(SAMPLES).astype(jnp.float32) - (side - 1) / 2.0
    base = (jnp.arange(per).astype(jnp.float32) + 0.5) / per - 0.5
    place = base[None, :] + shear_one * centred[:, None]
    whole = jnp.floor(place)
    part = place - whole
    reach = jnp.arange(TAPS).astype(jnp.float32) - 1.0
    weight = spline(part[:, :, None] - reach)
    weight = weight.astype(jnp.bfloat16).astype(jnp.float32)
    cell = whole[:, :, None] + reach
    return jnp.concatenate([weight, cell], 2).reshape(SAMPLES * per * 2 * TAPS)


def band(taps, at, offsets, odd):
    def value(index):
        even_one = taps[at + index]
        odd_one = taps[at + 2 * TAPS + index]
        return jnp.where(odd, odd_one, even_one).astype(jnp.bfloat16)

    result = jnp.zeros(offsets.shape, jnp.bfloat16)
    for tap in range(TAPS):
        result = jnp.where(offsets == value(TAPS + tap)[None], value(tap)[None], result)
    return result


def render_kernel(
    volume,
    row_taps,
    col_taps,
    scalars,
    rows_live,
    target,
    perm,
    owner,
    outgoing,
    slots,
    row_off,
    col_off,
    field_a,
    field_b,
    state,
    dealt,
    place,
):
    side = volume.shape[0]
    per = RAYS // side
    first = jnp.float32(jnp.bfloat16(2.0 / 3.0))
    second = jnp.float32(jnp.bfloat16(1.0 / 6.0))
    rate = scalars[0]
    slope = [scalars[1 + k] * 0.5 for k in range(3)]
    bias = [scalars[4 + k] * 0.5 for k in range(3)]

    row_shape = (RAYS // 16, 16, side)
    ray = lax.broadcasted_iota(jnp.int32, row_shape, 0) * 16 + lax.broadcasted_iota(
        jnp.int32, row_shape, 1
    )
    cell = lax.broadcasted_iota(jnp.int32, row_shape, 2)
    row_off[...] = (cell - ray // per).astype(jnp.float32).astype(jnp.bfloat16)
    col_shape = (side // 16, 16, RAYS)
    cell = lax.broadcasted_iota(jnp.int32, col_shape, 0) * 16 + lax.broadcasted_iota(
        jnp.int32, col_shape, 1
    )
    ray = lax.broadcasted_iota(jnp.int32, col_shape, 2)
    col_off[...] = (cell - ray // per).astype(jnp.float32).astype(jnp.bfloat16)
    row_odd = lax.broadcasted_iota(jnp.int32, (16, side), 0) % per == 1
    col_odd = lax.broadcasted_iota(jnp.int32, (16, RAYS), 1) % per == 1

    state[0] = jnp.ones((RAYS, RAYS), jnp.float32)
    for k in range(3):
        state[1 + k] = jnp.zeros((RAYS, RAYS), jnp.float32)

    def fields(start, out):
        last = SAMPLES - 1
        slices = [
            volume[jnp.clip(start + j - 1, 0, last)].astype(jnp.float32) for j in range(GROUP + 2)
        ]
        for j in range(GROUP):
            sample = jnp.minimum(start + j, last)
            below = jnp.where(sample == 0, 0.0, second)
            above = jnp.where(sample == last, 0.0, second)
            part = slices[j] * below + slices[j + 1] * first + slices[j + 2] * above
            part = part.astype(jnp.bfloat16)
            at = sample * (per * 2 * TAPS)
            row_table = band(row_taps, at, row_off[...], row_odd).reshape(RAYS, side)
            col_table = band(col_taps, at, col_off[...], col_odd).reshape(side, RAYS)
            half_way = jnp.dot(row_table, part, preferred_element_type=jnp.float32)
            out[j] = jnp.dot(
                half_way.astype(jnp.bfloat16), col_table, preferred_element_type=jnp.float32
            )

    def integrate(source):
        for tile in range(RAYS // ROWS):
            rows = slice(tile * ROWS, (tile + 1) * ROWS)
            clear = state[0, rows]
            colors = [state[1 + k, rows] for k in range(3)]
            for j in range(GROUP):
                field = source[j, rows]
                soft = jnp.log2(1.0 + jnp.exp2(field * LOG2E))
                after = clear * jnp.exp2(soft * -rate)
                weight = clear - after
                clear = after
                colors = [
                    colors[k] + weight * jnp.tanh(field * slope[k] + bias[k]) for k in range(3)
                ]
            state[0, rows] = clear
            for k in range(3):
                state[1 + k, rows] = colors[k]

    fields(0, field_a)

    def step(index, carry):
        start = index * (2 * GROUP)
        fields(start + GROUP, field_b)
        integrate(field_a)
        fields(start + 2 * GROUP, field_a)
        integrate(field_b)
        return carry

    lax.fori_loop(0, SAMPLES // (2 * GROUP), step, 0)

    groups = owner.shape[0]
    per_side = RAYS // FRAG
    count = per_side * per_side
    for t in range(groups):
        dealt[t] = 0
        for p in range(POS):
            slots[t, 0, p] = -1
    for f in range(count):
        tile = target[f]
        rank = dealt[tile]
        dealt[tile] = rank + 1
        receiver = owner[tile]
        slots[receiver, 0, perm[tile * POS + rank]] = rank
        place[f] = receiver * CAP + rank
    if groups * CAP > count:
        outgoing[...] = jnp.zeros(outgoing.shape, outgoing.dtype)

    row = lax.broadcasted_iota(jnp.int32, (FRAG, 2 * FRAG), 0)
    low = lax.broadcasted_iota(jnp.int32, (FRAG, 2 * FRAG), 1) < FRAG
    for fu in range(per_side):
        for pair in range(per_side // 2):
            f = fu * per_side + 2 * pair
            keep = row < jnp.where(low, rows_live[f], rows_live[f + 1])
            rows = slice(fu * FRAG, (fu + 1) * FRAG)
            lanes = slice(pair * 2 * FRAG, (pair + 1) * 2 * FRAG)
            alpha = 1.0 - state[0, rows, lanes]
            parts = [0.5 * (alpha + state[1 + k, rows, lanes]) for k in range(3)] + [alpha]
            parts = [jnp.where(keep, part, 0.0) for part in parts]
            turned = [pltpu.roll(part, FRAG, 1) for part in parts]
            for c in range(2):
                even = jnp.where(low, parts[2 * c], turned[2 * c + 1])
                odd = jnp.where(low, turned[2 * c], parts[2 * c + 1])
                outgoing[place[f], c] = even.astype(jnp.bfloat16)
                outgoing[place[f + 1], c] = odd.astype(jnp.bfloat16)


def render(brick, shear_pair, rate, color_slope, color_bias, rows_live, target, perm, owner):
    side = brick.shape[0]
    groups = owner.shape[0]
    smem = pl.BlockSpec(memory_space=pltpu.SMEM)
    vmem = pl.BlockSpec(memory_space=pltpu.VMEM)
    scalars = jnp.concatenate([rate[None], color_slope, color_bias, jnp.zeros((1,), jnp.float32)])
    return pl.pallas_call(
        render_kernel,
        out_shape=(
            jax.ShapeDtypeStruct((groups * CAP, 2, FRAG, 2 * FRAG), jnp.bfloat16),
            jax.ShapeDtypeStruct((groups, 8, 128), jnp.int32),
        ),
        in_specs=[vmem] + [smem] * 7,
        out_specs=(vmem, smem),
        scratch_shapes=[
            pltpu.VMEM((RAYS // 16, 16, side), jnp.bfloat16),
            pltpu.VMEM((side // 16, 16, RAYS), jnp.bfloat16),
            pltpu.VMEM((GROUP, RAYS, RAYS), jnp.float32),
            pltpu.VMEM((GROUP, RAYS, RAYS), jnp.float32),
            pltpu.VMEM((4, RAYS, RAYS), jnp.float32),
            pltpu.SMEM((groups,), jnp.int32),
            pltpu.SMEM(((RAYS // FRAG) ** 2,), jnp.int32),
        ],
        compiler_params=pltpu.CompilerParams(vmem_limit_bytes=32 * 2**20),
        cost_estimate=pl.CostEstimate(
            flops=2 * SAMPLES * RAYS * side * (side + RAYS),
            bytes_accessed=brick.size * 2,
            transcendentals=6 * SAMPLES * RAYS * RAYS,
        ),
        name="render",
    )(
        brick,
        taps_of(shear_pair[0], side),
        taps_of(shear_pair[1], side),
        scalars,
        rows_live,
        target,
        perm,
        owner,
    )


def over(front, back):
    veil = 1.0 - front[3:4]
    return jnp.concatenate([front[:3] + veil * back[:3], front[3:4] + veil * back[3:4]], 0)


def compose_kernel(
    outgoing,
    slots,
    view,
    owner,
    result,
    got,
    got_slots,
    slot_of,
    layer,
    given,
    taken,
    send_sem,
    recv_sem,
    note_send,
    note_recv,
    local_sem,
    swap_send,
    swap_recv,
    join_send,
    join_recv,
):
    groups = owner.shape[0]
    slabs = lax.axis_size("depth")
    levels = slabs.bit_length() - 1
    column = lax.axis_index("tile")
    slab = lax.axis_index("depth")
    mesh_id = pl.DeviceIdType.MESH

    def bit(level):
        return (slab // 2**level) % 2

    def partner(level):
        return (column, slab + 2**level * (1 - 2 * bit(level)))

    barrier = pltpu.get_barrier_semaphore()
    for j in range(1, groups):
        there = (lax.rem(column + j, groups), slab)
        pl.semaphore_signal(barrier, inc=1, device_id=there, device_id_type=mesh_id)
    for level in range(levels):
        pl.semaphore_signal(barrier, inc=1, device_id=partner(level), device_id_type=mesh_id)
    pl.semaphore_wait(barrier, groups - 1 + levels)

    def note_copy(j, source):
        peer = lax.rem(column + j, groups)
        return pltpu.make_async_remote_copy(
            src_ref=slots.at[peer],
            dst_ref=got_slots.at[source],
            send_sem=note_send.at[j],
            recv_sem=note_recv.at[source],
            device_id=(peer, slab),
            device_id_type=mesh_id,
        )

    def frag_copy(j, source):
        peer = lax.rem(column + j, groups)
        return pltpu.make_async_remote_copy(
            src_ref=outgoing.at[pl.ds(peer * CAP, CAP)],
            dst_ref=got.at[pl.ds(source * CAP, CAP)],
            send_sem=send_sem.at[j],
            recv_sem=recv_sem.at[source],
            device_id=(peer, slab),
            device_id_type=mesh_id,
        )

    for j in range(1, groups):
        note_copy(j, column).start()
    for j in range(1, groups):
        frag_copy(j, column).start()
    own_note = pltpu.make_async_copy(slots.at[column], got_slots.at[column], local_sem.at[0])
    own_frags = pltpu.make_async_copy(
        outgoing.at[pl.ds(column * CAP, CAP)], got.at[pl.ds(column * CAP, CAP)], local_sem.at[1]
    )
    own_note.start()
    own_frags.start()
    own_note.wait()
    for j in range(1, groups):
        note_copy(j, lax.rem(column + groups - j, groups)).wait()
    to_scalar = pltpu.make_async_copy(got_slots, slot_of, local_sem.at[2])
    to_scalar.start()
    to_scalar.wait()
    own_frags.wait()
    for j in range(1, groups):
        frag_copy(j, lax.rem(column + groups - j, groups)).wait()

    mine_view = jnp.int32(0)
    for t in range(groups):
        mine_view = jnp.where(owner[t] == column, view[t], mine_view)

    low = lax.broadcasted_iota(jnp.int32, (FRAG, 2 * FRAG), 1) < FRAG
    per_tile = TILE_SIDE // FRAG

    def landed(position):
        def one(source, total):
            slot = slot_of[source, 0, position]
            block = got[source * CAP + jnp.maximum(slot, 0)].astype(jnp.float32)
            return total + jnp.where(slot >= 0, block, 0.0)

        total = jnp.zeros((2, FRAG, 2 * FRAG), jnp.float32)
        if groups <= 4:
            for source in range(groups):
                total = one(source, total)
            return total
        return lax.fori_loop(0, groups, one, total)

    def lay(frag_row, store):
        for pair in range(per_tile // 2):
            left = landed(frag_row * per_tile + 2 * pair)
            right = landed(frag_row * per_tile + 2 * pair + 1)
            lanes = slice(pair * 2 * FRAG, (pair + 1) * 2 * FRAG)
            for c in range(2):
                store(2 * c, lanes, jnp.where(low, left[c], pltpu.roll(right[c], FRAG, 1)))
                store(2 * c + 1, lanes, jnp.where(low, pltpu.roll(left[c], FRAG, 1), right[c]))

    half = TILE_SIDE // 2
    rows_in_half = half // FRAG

    def lay_given(step, carry):
        def store(channel, lanes, value):
            given[channel, pl.ds(step * FRAG, FRAG), lanes] = value.astype(jnp.bfloat16)

        lay((1 - bit(0)) * rows_in_half + step, store)
        return carry

    def lay_kept(step, carry):
        def store(channel, lanes, value):
            layer[channel, pl.ds(step * FRAG, FRAG), lanes] = value

        lay(bit(0) * rows_in_half + step, store)
        return carry

    def swap(level, height, at):
        return pltpu.make_async_remote_copy(
            src_ref=given.at[:, pl.ds(at, height)],
            dst_ref=taken.at[:, pl.ds(at, height)],
            send_sem=swap_send.at[level],
            recv_sem=swap_recv.at[level],
            device_id=partner(level),
            device_id_type=mesh_id,
        )

    lax.fori_loop(0, rows_in_half, lay_given, 0)
    first = swap(0, half, 0)
    first.start()
    lax.fori_loop(0, rows_in_half, lay_kept, 0)

    chunk = 16
    copy = first
    height = half
    at = 0
    start = 0
    offset = bit(0) * half
    for level in range(levels):
        copy.wait()
        mine_front = (bit(level) + mine_view) % 2 == 0
        last = level == levels - 1

        def blend(from_row, count, put, mine_front=mine_front, at=at, start=start):
            def step(index, carry):
                row = pl.multiple_of(from_row + index * chunk, chunk)
                mine = layer[:, pl.ds(start + row, chunk)]
                other = taken[:, pl.ds(at + row, chunk)].astype(jnp.float32)
                front = jnp.where(mine_front, mine, other)
                back = jnp.where(mine_front, other, mine)
                put(pl.multiple_of(index * chunk, chunk), over(front, back))
                return carry

            lax.fori_loop(0, count // chunk, step, 0)

        if last:

            def put_result(row, value, offset=offset):
                result[:, pl.ds(pl.multiple_of(offset + row, chunk), chunk)] = value.astype(
                    jnp.bfloat16
                )

            blend(0, height, put_result)
        else:
            lower = height // 2
            after = at + height

            def put_given(row, value, after=after):
                given[:, pl.ds(pl.multiple_of(after + row, chunk), chunk)] = value.astype(
                    jnp.bfloat16
                )

            def put_kept(row, value, base=half * 2 - height):
                layer[:, pl.ds(pl.multiple_of(base + row, chunk), chunk)] = value

            blend((1 - bit(level + 1)) * lower, lower, put_given)
            copy = swap(level + 1, lower, after)
            copy.start()
            blend(bit(level + 1) * lower, lower, put_kept)
            start = half * 2 - height
            offset = offset + bit(level + 1) * lower
            at = after
            height = lower

    for level in reversed(range(levels)):
        rows = pl.ds(pl.multiple_of(offset, chunk), height)
        join = pltpu.make_async_remote_copy(
            src_ref=result.at[:, rows],
            dst_ref=result.at[:, rows],
            send_sem=join_send.at[level],
            recv_sem=join_recv.at[level],
            device_id=partner(level),
            device_id_type=mesh_id,
        )
        join.start()
        join.wait()
        offset = offset - bit(level) * height
        height = height * 2


def compose(outgoing, slots, tile_view, tile_owner):
    groups = tile_owner.shape[0]
    levels = lax.axis_size("depth").bit_length() - 1
    smem = pl.BlockSpec(memory_space=pltpu.SMEM)
    vmem = pl.BlockSpec(memory_space=pltpu.VMEM)
    dma = pltpu.SemaphoreType.DMA
    return pl.pallas_call(
        compose_kernel,
        out_shape=jax.ShapeDtypeStruct((4, TILE_SIDE, TILE_SIDE), jnp.bfloat16),
        in_specs=[vmem, vmem, smem, smem],
        out_specs=vmem,
        scratch_shapes=[
            pltpu.VMEM(outgoing.shape, jnp.bfloat16),
            pltpu.VMEM(slots.shape, jnp.int32),
            pltpu.SMEM(slots.shape, jnp.int32),
            pltpu.VMEM((4, TILE_SIDE, TILE_SIDE), jnp.float32),
            pltpu.VMEM((4, TILE_SIDE, TILE_SIDE), jnp.bfloat16),
            pltpu.VMEM((4, TILE_SIDE, TILE_SIDE), jnp.bfloat16),
            dma((groups,)),
            dma((groups,)),
            dma((groups,)),
            dma((groups,)),
            dma((3,)),
            dma((levels,)),
            dma((levels,)),
            dma((levels,)),
            dma((levels,)),
        ],
        compiler_params=pltpu.CompilerParams(
            collective_id=0, has_side_effects=True, vmem_limit_bytes=32 * 2**20
        ),
        cost_estimate=pl.CostEstimate(
            flops=2**24, bytes_accessed=2 * outgoing.size, transcendentals=0
        ),
        name="compose",
    )(outgoing, slots, tile_view, tile_owner)


def local(
    volume,
    shear,
    absorb,
    color_slope,
    color_bias,
    frag_tile,
    slot_perm,
    frag_rows,
    tile_view,
    tile_owner,
):
    outgoing, slots = render(
        volume[0, 0],
        shear[0, 0],
        absorb[0, 0],
        color_slope,
        color_bias,
        frag_rows[0, 0],
        frag_tile[0, 0, :, 0],
        slot_perm[0, 0].reshape(-1),
        tile_owner,
    )
    return compose(outgoing, slots, tile_view, tile_owner)[None]


def solution(mesh):
    in_specs = (
        P("tile", "depth", None, None, None),
        P("tile", "depth", None),
        P("tile", "depth"),
        P(),
        P(),
        P("tile", "depth", None, None),
        P("tile", "depth", None, None),
        P("tile", "depth", None),
        P(),
        P(),
    )
    out_specs = P("tile", None, None, None)
    return jax.shard_map(local, mesh=mesh, in_specs=in_specs, out_specs=out_specs, check_vma=False)
```

profile of v0, /device:TPU:0, one launch (start us, length us, event | category | flops | bytes accessed | tf_op | source)
XLA Modules:
  0.0 89.2 jit_solution(18115620698378860837)
XLA Ops:
  0.7 0.8 pad_maximum_fusion.2.scalars
  1.4 0.8 reshape_squeeze.3.perm
  2.2 1.3 %fusion.22 = (f32[1,1,1]{2,1,0:T(1,128)}, f32[1,1,1]{2,1,0:T(1,128)}) fusion(f32[1,1,2]{2,1,0:T(1,128)} %param.11), kind=kLoop, calls=%fused_computation.42 | loop fusion | bytes 16 | tf_op jit(solution)/shard_map/slice | solution.py:219
  3.5 1.3 %fusion.20 = (f32[128]{0:T(128)S(1)}, f32[128]{0:T(128)S(1)}) fusion(f32[]{:T(128)} %bitcast.2, f32[]{:T(128)} %bitcast.1), kind=kLoop, calls=%fused_computation.39 | loop fusion | flops 512 | bytes 1032 | tf_op jit(solution)/shard_map/mul | solution.py:33
  4.8 0.1 add_subtract_fusion
  4.8 0.1 fusion.18
  5.0 0.1 copy.11
  5.1 0.2 reshape.143.row_taps
  5.3 0.1 copy.12
  5.5 0.2 reshape.144.col_taps
  5.7 0.0 copy-start
  5.7 0.7 copy-done
  6.3 0.0 copy-start.2
  6.3 2.2 %copy-done.2 = bf16[1,1,128,128,128]{4,3,2,1,0:T(8,128)(2,1)S(1)} copy-done((bf16[1,1,128,128,128]{4,3,2,1,0:T(8,128)(2,1)S(1)}, bf16[1,1,128,128,128]{4,3,2,1,0:T(8,128)(2,1)}, u32[]{:S(2)}) %copy-start.2) | copy-done | bytes 4194328
  8.5 0.0 copy-start.3
  8.5 0.7 copy-done.3
  9.2 0.0 copy-start.4
  9.2 0.7 copy-done.4
  9.8 0.0 copy-start.1
  9.8 44.6 %render.1 = (bf16[16,2,64,128]{3,2,1,0:T(8,128)(2,1)S(1)}, s32[4,8,128]{2,1,0:T(8,128)S(1)}) custom-call(bf16[128,128,128]{2,1,0:T(8,128)(2,1)S(1)} %bitcast.9, f32[2048]{0:T(1024)S(1)} %reshape.143.row_taps, f32[2048]{0:T(1024)S(1)} %reshape.144.col_taps, f32[8]{0:T(128)S(1)} %pad_maximum_fusion.2.scalars, s32[16]{0:T(128)S(1)} %bitcast.10, ...), custom_call_target="tpu_custom_call" | custom-call | flops 3221225472 | bytes 4194304 | tf_op jit(solution)/shard_map/render/pallas_call | solution.py:192
  54.4 0.0 copy-done.1
  54.4 34.0 %compose.1 = bf16[4,256,256]{2,1,0:T(8,128)(2,1)S(1)} custom-call(bf16[16,2,64,128]{3,2,1,0:T(8,128)(2,1)S(1)} %get-tuple-element.7.outgoing, s32[4,8,128]{2,1,0:T(8,128)S(1)} %get-tuple-element.8.slots, s32[4]{0:T(128)S(1)} %copy-done.1, s32[4]{0:T(128)S(1)} %copy-done), custom_call_target="tpu_custom_call" | custom-call | flops 16777216 | bytes 524288 | tf_op jit(solution)/shard_map/compose/pallas_call | solution.py:453
  88.4 0.8 copy.15
  (4 shorter events, 0.0 us)
Async XLA Ops:
  5.7 0.7 copy-start
  6.3 2.2 %copy-start.2 = (bf16[1,1,128,128,128]{4,3,2,1,0:T(8,128)(2,1)S(1)}, bf16[1,1,128,128,128]{4,3,2,1,0:T(8,128)(2,1)}, u32[]{:S(2)}) copy-start(bf16[1,1,128,128,128]{4,3,2,1,0:T(8,128)(2,1)} %param.10) | copy-start | bytes 12582916
  8.5 0.7 copy-start.3
  9.2 0.7 copy-start.4
  9.8 44.6 %copy-start.1 = (s32[4]{0:T(128)S(1)}, s32[4]{0:T(128)}, u32[]{:S(2)}) copy-start(s32[4]{0:T(128)} %view.1) | copy-start | bytes 52
where the time goes:
time: 89.5 us; the launch traced here: 89.2 us
  Pallas kernels  78.6 us (88%)
  local copies, waits for them, and re-layouts  7.74 us (9%)
  other arithmetic  2.21 us (2%)
    pallas_call x1, Pallas kernels, render(): pl.pallas_call(render_kernel, out_shape=(jax.ShapeDtypeStruct((groups * C...  44.6 us
    pallas_call x1, Pallas kernels, compose(): pl.pallas_call(compose_kernel, out_shape=jax.ShapeDtypeStruct((4, TILE_SI...  34 us
    unnamed x11, local copies, waits for them, and re-layouts  4.96 us

commit v1 on v0

v1 whole, which is shorter than its diff:
```python
import functools
import jax
import jax.numpy as jnp
from jax import lax
from jax.experimental import pallas as pl
from jax.experimental.pallas import tpu as pltpu
from jax.sharding import PartitionSpec as P

SAMPLES = 128
RAYS = 256
FRAG = 64
TILE_SIDE = 256
CAP = 4
POS = 16
GROUP = 4
ROWS = 16
TAPS = 4
LOG2E = 1.4426950408889634


def spline(offset):
    size_abs = jnp.abs(offset)
    inner = 2.0 / 3.0 - size_abs * size_abs + 0.5 * size_abs * size_abs * size_abs
    remain = 2.0 - size_abs
    outer = remain * remain * remain / 6.0
    return jnp.where(size_abs < 1.0, inner, jnp.where(size_abs < 2.0, outer, 0.0))


def taps_of(shear, side):
    per = RAYS // side
    shape = (SAMPLES, 128)
    sample = lax.broadcasted_iota(jnp.int32, shape, 0).astype(jnp.float32)
    lane = lax.broadcasted_iota(jnp.int32, shape, 1)
    parity = ((lane // (2 * TAPS)) % per).astype(jnp.float32)
    reach = (lane % TAPS).astype(jnp.float32) - 1.0
    base = (parity + 0.5) / per - 0.5
    shift = jnp.where((lane // (2 * TAPS * per)) % 2 == 0, shear[0, 0, 0], shear[0, 0, 1])
    place = base + shift * (sample - (side - 1) / 2.0)
    whole = jnp.floor(place)
    weight = spline(place - whole - reach)
    return jnp.where((lane // TAPS) % 2 == 0, weight, whole + reach)


def band(taps, sample, at, offsets, odd):
    def value(index):
        even_one = taps[sample, at + index]
        odd_one = taps[sample, at + 2 * TAPS + index]
        return jnp.where(odd, odd_one, even_one).astype(jnp.bfloat16)

    result = jnp.zeros(offsets.shape, jnp.bfloat16)
    for tap in range(TAPS):
        result = jnp.where(offsets == value(TAPS + tap)[None], value(tap)[None], result)
    return result


def render_kernel(
    brick,
    shear,
    absorb,
    color_slope,
    color_bias,
    rows_live,
    target,
    perm,
    owner,
    outgoing,
    slots,
    row_off,
    col_off,
    field_a,
    field_b,
    state,
    dealt,
    place,
    volume,
    taps_wide,
    taps,
    copy_sem,
):
    side = brick.shape[2]
    head = 4 * GROUP
    bring_head = pltpu.make_async_copy(
        brick.at[0, 0, pl.ds(0, head)], volume.at[pl.ds(0, head)], copy_sem.at[0]
    )
    bring_rest = pltpu.make_async_copy(
        brick.at[0, 0, pl.ds(head, side - head)],
        volume.at[pl.ds(head, side - head)],
        copy_sem.at[1],
    )
    bring_head.start()
    bring_rest.start()
    taps_wide[...] = taps_of(shear, side)
    bring_taps = pltpu.make_async_copy(taps_wide, taps, copy_sem.at[2])
    bring_taps.start()
    per = RAYS // side
    first = jnp.float32(jnp.bfloat16(2.0 / 3.0))
    second = jnp.float32(jnp.bfloat16(1.0 / 6.0))
    fade = absorb[0, 0] * -LOG2E
    slope = [color_slope[k] * 0.5 for k in range(3)]
    bias = [color_bias[k] * 0.5 for k in range(3)]

    row_shape = (RAYS // 16, 16, side)
    ray = lax.broadcasted_iota(jnp.int32, row_shape, 0) * 16 + lax.broadcasted_iota(
        jnp.int32, row_shape, 1
    )
    cell = lax.broadcasted_iota(jnp.int32, row_shape, 2)
    row_off[...] = (cell - ray // per).astype(jnp.float32).astype(jnp.bfloat16)
    col_shape = (side // 16, 16, RAYS)
    cell = lax.broadcasted_iota(jnp.int32, col_shape, 0) * 16 + lax.broadcasted_iota(
        jnp.int32, col_shape, 1
    )
    ray = lax.broadcasted_iota(jnp.int32, col_shape, 2)
    col_off[...] = (cell - ray // per).astype(jnp.float32).astype(jnp.bfloat16)
    row_odd = lax.broadcasted_iota(jnp.int32, (16, side), 0) % per == 1
    col_odd = lax.broadcasted_iota(jnp.int32, (16, RAYS), 1) % per == 1

    state[0] = jnp.ones((RAYS, RAYS), jnp.float32)
    for k in range(3):
        state[1 + k] = jnp.zeros((RAYS, RAYS), jnp.float32)

    def fields(start, out):
        last = SAMPLES - 1
        slices = [
            volume[jnp.clip(start + j - 1, 0, last)].astype(jnp.float32) for j in range(GROUP + 2)
        ]
        for j in range(GROUP):
            sample = jnp.minimum(start + j, last)
            below = jnp.where(sample == 0, 0.0, second)
            above = jnp.where(sample == last, 0.0, second)
            part = slices[j] * below + slices[j + 1] * first + slices[j + 2] * above
            part = part.astype(jnp.bfloat16)
            row_table = band(taps, sample, 0, row_off[...], row_odd).reshape(RAYS, side)
            col_table = band(taps, sample, 2 * TAPS * per, col_off[...], col_odd).reshape(side, RAYS)
            half_way = jnp.dot(row_table, part, preferred_element_type=jnp.float32)
            out[j] = jnp.dot(
                half_way.astype(jnp.bfloat16), col_table, preferred_element_type=jnp.float32
            )

    def integrate(source):
        for tile in range(RAYS // ROWS):
            rows = slice(tile * ROWS, (tile + 1) * ROWS)
            clear = state[0, rows]
            colors = [state[1 + k, rows] for k in range(3)]
            for j in range(GROUP):
                field = source[j, rows]
                soft = jnp.log(1.0 + jnp.exp2(field * LOG2E))
                after = clear * jnp.exp2(soft * fade)
                weight = clear - after
                clear = after
                colors = [
                    colors[k] + weight * jnp.tanh(field * slope[k] + bias[k]) for k in range(3)
                ]
            state[0, rows] = clear
            for k in range(3):
                state[1 + k, rows] = colors[k]

    bring_taps.wait()
    bring_head.wait()
    fields(0, field_a)

    def step(index, carry):
        start = index * (2 * GROUP)

        @pl.when(index == 1)
        def rest_is_here():
            bring_rest.wait()

        fields(start + GROUP, field_b)
        integrate(field_a)
        fields(start + 2 * GROUP, field_a)
        integrate(field_b)
        return carry

    lax.fori_loop(0, SAMPLES // (2 * GROUP), step, 0)

    groups = owner.shape[0]
    per_side = RAYS // FRAG
    count = per_side * per_side
    for t in range(groups):
        dealt[t] = 0
        for p in range(POS):
            slots[t, 0, p] = -1
    for f in range(count):
        tile = target[0, 0, f, 0]
        rank = dealt[tile]
        dealt[tile] = rank + 1
        receiver = owner[tile]
        slots[receiver, 0, perm[0, 0, tile, rank]] = rank
        place[f] = receiver * CAP + rank
    if groups * CAP > count:
        outgoing[...] = jnp.zeros(outgoing.shape, outgoing.dtype)

    row = lax.broadcasted_iota(jnp.int32, (FRAG, 2 * FRAG), 0)
    low = lax.broadcasted_iota(jnp.int32, (FRAG, 2 * FRAG), 1) < FRAG
    for fu in range(per_side):
        for pair in range(per_side // 2):
            f = fu * per_side + 2 * pair
            keep = row < jnp.where(low, rows_live[0, 0, f], rows_live[0, 0, f + 1])
            rows = slice(fu * FRAG, (fu + 1) * FRAG)
            lanes = slice(pair * 2 * FRAG, (pair + 1) * 2 * FRAG)
            alpha = 1.0 - state[0, rows, lanes]
            parts = [0.5 * (alpha + state[1 + k, rows, lanes]) for k in range(3)] + [alpha]
            parts = [jnp.where(keep, part, 0.0) for part in parts]
            turned = [pltpu.roll(part, FRAG, 1) for part in parts]
            for c in range(2):
                even = jnp.where(low, parts[2 * c], turned[2 * c + 1])
                odd = jnp.where(low, turned[2 * c], parts[2 * c + 1])
                outgoing[place[f], c] = even.astype(jnp.bfloat16)
                outgoing[place[f + 1], c] = odd.astype(jnp.bfloat16)


def render(brick, shear, absorb, color_slope, color_bias, rows_live, target, perm, owner):
    side = brick.shape[2]
    groups = owner.shape[0]
    smem = pl.BlockSpec(memory_space=pltpu.SMEM)
    vmem = pl.BlockSpec(memory_space=pltpu.VMEM)
    return pl.pallas_call(
        render_kernel,
        out_shape=(
            jax.ShapeDtypeStruct((groups * CAP, 2, FRAG, 2 * FRAG), jnp.bfloat16),
            jax.ShapeDtypeStruct((groups, 8, 128), jnp.int32),
        ),
        in_specs=[pl.BlockSpec(memory_space=pl.ANY)] + [smem] * 8,
        out_specs=(vmem, smem),
        scratch_shapes=[
            pltpu.VMEM((RAYS // 16, 16, side), jnp.bfloat16),
            pltpu.VMEM((side // 16, 16, RAYS), jnp.bfloat16),
            pltpu.VMEM((GROUP, RAYS, RAYS), jnp.float32),
            pltpu.VMEM((GROUP, RAYS, RAYS), jnp.float32),
            pltpu.VMEM((4, RAYS, RAYS), jnp.float32),
            pltpu.SMEM((groups,), jnp.int32),
            pltpu.SMEM(((RAYS // FRAG) ** 2,), jnp.int32),
            pltpu.VMEM((side, side, side), jnp.bfloat16),
            pltpu.VMEM((SAMPLES, 128), jnp.float32),
            pltpu.SMEM((SAMPLES, 128), jnp.float32),
            pltpu.SemaphoreType.DMA((3,)),
        ],
        compiler_params=pltpu.CompilerParams(vmem_limit_bytes=56 * 2**20),
        cost_estimate=pl.CostEstimate(
            flops=2 * SAMPLES * RAYS * side * (side + RAYS),
            bytes_accessed=brick.size * 2,
            transcendentals=6 * SAMPLES * RAYS * RAYS,
        ),
        name="render",
    )(brick, shear, absorb, color_slope, color_bias, rows_live, target, perm, owner)


def over(front, back):
    veil = 1.0 - front[3:4]
    return jnp.concatenate([front[:3] + veil * back[:3], front[3:4] + veil * back[3:4]], 0)


def compose_kernel(
    outgoing,
    slots,
    view,
    owner,
    result,
    got_first,
    got_second,
    got_slots,
    slot_of,
    layer,
    given,
    taken,
    send_sem,
    recv_sem,
    note_send,
    note_recv,
    local_sem,
    swap_send,
    swap_recv,
    join_send,
    join_recv,
):
    groups = owner.shape[0]
    slabs = lax.axis_size("depth")
    levels = slabs.bit_length() - 1
    column = lax.axis_index("tile")
    slab = lax.axis_index("depth")
    mesh_id = pl.DeviceIdType.MESH

    def bit(level):
        return (slab // 2**level) % 2

    def partner(level):
        return (column, slab + 2**level * (1 - 2 * bit(level)))

    barrier = pltpu.get_barrier_semaphore()
    for j in range(1, groups):
        there = (lax.rem(column + j, groups), slab)
        pl.semaphore_signal(barrier, inc=1, device_id=there, device_id_type=mesh_id)
    for level in range(levels):
        pl.semaphore_signal(barrier, inc=1, device_id=partner(level), device_id_type=mesh_id)
    pl.semaphore_wait(barrier, groups - 1 + levels)

    def note_copy(j, source):
        peer = lax.rem(column + j, groups)
        return pltpu.make_async_remote_copy(
            src_ref=slots.at[peer],
            dst_ref=got_slots.at[source],
            send_sem=note_send.at[j],
            recv_sem=note_recv.at[source],
            device_id=(peer, slab),
            device_id_type=mesh_id,
        )

    chunks = given.shape[0]
    got = (got_first, got_second)
    part = FRAG // chunks
    rows_all = TILE_SIDE // chunks

    def frag_copy(chunk, j, source):
        peer = lax.rem(column + j, groups)
        rows = pl.ds(chunk * part, part)
        return pltpu.make_async_remote_copy(
            src_ref=outgoing.at[pl.ds(peer * CAP, CAP), :, rows],
            dst_ref=got[chunk].at[pl.ds(source * CAP, CAP)],
            send_sem=send_sem.at[chunk, j],
            recv_sem=recv_sem.at[chunk, source],
            device_id=(peer, slab),
            device_id_type=mesh_id,
        )

    for j in range(1, groups):
        note_copy(j, column).start()
    for chunk in range(chunks):
        for j in range(1, groups):
            frag_copy(chunk, j, column).start()
    own_note = pltpu.make_async_copy(slots.at[column], got_slots.at[column], local_sem.at[0])
    own_frags = [
        pltpu.make_async_copy(
            outgoing.at[pl.ds(column * CAP, CAP), :, pl.ds(chunk * part, part)],
            got[chunk].at[pl.ds(column * CAP, CAP)],
            local_sem.at[2 + chunk],
        )
        for chunk in range(chunks)
    ]
    own_note.start()
    for own in own_frags:
        own.start()
    own_note.wait()
    for j in range(1, groups):
        note_copy(j, lax.rem(column + groups - j, groups)).wait()
    to_scalar = pltpu.make_async_copy(got_slots, slot_of, local_sem.at[1])
    to_scalar.start()
    to_scalar.wait()
    for own in own_frags:
        own.wait()

    mine_view = jnp.int32(0)
    for t in range(groups):
        mine_view = jnp.where(owner[t] == column, view[t], mine_view)

    low = lax.broadcasted_iota(jnp.int32, (part, 2 * FRAG), 1) < FRAG
    per_tile = TILE_SIDE // FRAG
    block = 16

    def landed(chunk, position):
        def one(source, total):
            slot = slot_of[source, 0, position]
            index = source * CAP + jnp.maximum(slot, 0)
            found = got[chunk][index].astype(jnp.float32)
            return total + jnp.where(slot >= 0, found, 0.0)

        total = jnp.zeros((2, part, 2 * FRAG), jnp.float32)
        if groups <= 4:
            for source in range(groups):
                total = one(source, total)
            return total
        return lax.fori_loop(0, groups, one, total)

    def lay(chunk, frag_row, store):
        for pair in range(per_tile // 2):
            left = landed(chunk, frag_row * per_tile + 2 * pair)
            right = landed(chunk, frag_row * per_tile + 2 * pair + 1)
            lanes = slice(pair * 2 * FRAG, (pair + 1) * 2 * FRAG)
            for c in range(2):
                store(2 * c, lanes, jnp.where(low, left[c], pltpu.roll(right[c], FRAG, 1)))
                store(2 * c + 1, lanes, jnp.where(low, pltpu.roll(left[c], FRAG, 1), right[c]))

    half = rows_all // 2
    frag_rows_half = per_tile // 2

    def swap(chunk, level, height, at):
        return pltpu.make_async_remote_copy(
            src_ref=given.at[chunk, :, pl.ds(at, height)],
            dst_ref=taken.at[chunk, :, pl.ds(at, height)],
            send_sem=swap_send.at[chunk, level],
            recv_sem=swap_recv.at[chunk, level],
            device_id=partner(level),
            device_id_type=mesh_id,
        )

    def spot(chunk, offset, height):
        if height >= part:
            return (
                slice(None),
                pl.ds(lax.div(offset, part), height // part),
                pl.ds(chunk * part, part),
            )
        row = pl.multiple_of(chunk * part + lax.rem(offset, part), block)
        return (slice(None), pl.ds(lax.div(offset, part), 1), pl.ds(row, height))

    def steps(chunk):
        for j in range(1, groups):
            frag_copy(chunk, j, lax.rem(column + groups - j, groups)).wait()

        def lay_given(step, carry):
            def store(channel, lanes, value):
                rows = pl.ds(pl.multiple_of(step * part, part), part)
                given[chunk, channel, rows, lanes] = value.astype(jnp.bfloat16)

            lay(chunk, (1 - bit(0)) * frag_rows_half + step, store)
            return carry

        def lay_kept(step, carry):
            def store(channel, lanes, value):
                rows = pl.ds(pl.multiple_of(step * part, part), part)
                layer[chunk, channel, rows, lanes] = value

            lay(chunk, bit(0) * frag_rows_half + step, store)
            return carry

        lax.fori_loop(0, frag_rows_half, lay_given, 0)
        copy = swap(chunk, 0, half, 0)
        copy.start()
        lax.fori_loop(0, frag_rows_half, lay_kept, 0)
        yield

        height = half
        at = 0
        start = 0
        offset = bit(0) * half
        for level in range(levels):
            copy.wait()
            mine_front = (bit(level) + mine_view) % 2 == 0

            def blend(from_row, count, put, mine_front=mine_front, at=at, start=start):
                def step(index, carry):
                    row = pl.multiple_of(from_row + index * block, block)
                    mine = layer[chunk, :, pl.ds(start + row, block)]
                    other = taken[chunk, :, pl.ds(at + row, block)].astype(jnp.float32)
                    front = jnp.where(mine_front, mine, other)
                    back = jnp.where(mine_front, other, mine)
                    put(pl.multiple_of(index * block, block), over(front, back))
                    return carry

                lax.fori_loop(0, count // block, step, 0)

            if level == levels - 1:

                def put_result(row, value, offset=offset):
                    where = spot(chunk, offset + row, block)
                    result[where] = value.astype(jnp.bfloat16)[:, None]

                blend(0, height, put_result)
                break
            lower = height // 2
            after = at + height
            below = rows_all - height

            def put_given(row, value, after=after):
                rows = pl.ds(pl.multiple_of(after + row, block), block)
                given[chunk, :, rows] = value.astype(jnp.bfloat16)

            def put_kept(row, value, below=below):
                layer[chunk, :, pl.ds(pl.multiple_of(below + row, block), block)] = value

            blend((1 - bit(level + 1)) * lower, lower, put_given)
            copy = swap(chunk, level + 1, lower, after)
            copy.start()
            blend(bit(level + 1) * lower, lower, put_kept)
            yield
            start = below
            offset = offset + bit(level + 1) * lower
            at = after
            height = lower

        for level in reversed(range(levels)):
            where = spot(chunk, offset, height)
            join = pltpu.make_async_remote_copy(
                src_ref=result.at[where],
                dst_ref=result.at[where],
                send_sem=join_send.at[chunk, level],
                recv_sem=join_recv.at[chunk, level],
                device_id=partner(level),
                device_id_type=mesh_id,
            )
            join.start()
            yield
            join.wait()
            offset = offset - bit(level) * height
            height = height * 2

    running = [steps(chunk) for chunk in range(chunks)]
    while running:
        running = [one for one in running if next(one, "done") != "done"]


def compose(outgoing, slots, tile_view, tile_owner):
    groups = tile_owner.shape[0]
    slabs = lax.axis_size("depth")
    levels = slabs.bit_length() - 1
    chunks = max(1, min(2, TILE_SIDE // (16 * slabs)))
    per_tile = TILE_SIDE // FRAG
    rows = TILE_SIDE // chunks
    smem = pl.BlockSpec(memory_space=pltpu.SMEM)
    vmem = pl.BlockSpec(memory_space=pltpu.VMEM)
    dma = pltpu.SemaphoreType.DMA
    return pl.pallas_call(
        compose_kernel,
        out_shape=jax.ShapeDtypeStruct((4, per_tile, FRAG, TILE_SIDE), jnp.bfloat16),
        in_specs=[vmem, vmem, smem, smem],
        out_specs=vmem,
        scratch_shapes=[
            pltpu.VMEM((groups * CAP, 2, FRAG // chunks, 2 * FRAG), jnp.bfloat16),
            pltpu.VMEM((groups * CAP, 2, FRAG // chunks, 2 * FRAG), jnp.bfloat16),
            pltpu.VMEM(slots.shape, jnp.int32),
            pltpu.SMEM(slots.shape, jnp.int32),
            pltpu.VMEM((chunks, 4, rows, TILE_SIDE), jnp.float32),
            pltpu.VMEM((chunks, 4, rows, TILE_SIDE), jnp.bfloat16),
            pltpu.VMEM((chunks, 4, rows, TILE_SIDE), jnp.bfloat16),
            dma((chunks, groups)),
            dma((chunks, groups)),
            dma((groups,)),
            dma((groups,)),
            dma((4,)),
            dma((chunks, levels)),
            dma((chunks, levels)),
            dma((chunks, levels)),
            dma((chunks, levels)),
        ],
        compiler_params=pltpu.CompilerParams(
            collective_id=0, has_side_effects=True, vmem_limit_bytes=32 * 2**20
        ),
        cost_estimate=pl.CostEstimate(
            flops=2**24, bytes_accessed=2 * outgoing.size, transcendentals=0
        ),
        name="compose",
    )(outgoing, slots, tile_view, tile_owner)


def local(
    volume,
    shear,
    absorb,
    color_slope,
    color_bias,
    frag_tile,
    slot_perm,
    frag_rows,
    tile_view,
    tile_owner,
):
    outgoing, slots = render(
        volume,
        shear,
        absorb,
        color_slope,
        color_bias,
        frag_rows,
        frag_tile,
        slot_perm,
        tile_owner,
    )
    frame = compose(outgoing, slots, tile_view, tile_owner)
    return frame.reshape(1, 4, TILE_SIDE, TILE_SIDE)


def solution(mesh):
    in_specs = (
        P("tile", "depth", None, None, None),
        P("tile", "depth", None),
        P("tile", "depth"),
        P(),
        P(),
        P("tile", "depth", None, None),
        P("tile", "depth", None, None),
        P("tile", "depth", None),
        P(),
        P(),
    )
    out_specs = P("tile", None, None, None)
    return jax.shard_map(local, mesh=mesh, in_specs=in_specs, out_specs=out_specs, check_vma=False)
```

time: 89.5 us -> 82.2 us (0.918)
  local copies, waits for them, and re-layouts: 7.74 us -> 3.88 us
  other arithmetic: 2.21 us -> 0 us
  Pallas kernels: 78.6 us -> 77.3 us
    pallas_call x1, Pallas kernels: 34 us -> 31.3 us  [compose(): pl.pallas_call(compose_kernel, out_shape=jax.ShapeDtypeStruct((4, per_til...]
    pallas_call x1, Pallas kernels: 44.6 us -> 46 us  [render(): pl.pallas_call(render_kernel, out_shape=(jax.ShapeDtypeStruct((groups * C...]
    slice x1 -> x0, local copies, waits for them, and re-layouts: 1.31 us -> none  [render(): shear_pair[1]]
    mul x1 -> x0, other arithmetic: 1.27 us -> none  [taps_of(): place = base[None, :] + shear_one * centred[:, None]]
    unnamed x11 -> x10, local copies, waits for them, and re-layouts: 4.96 us -> 3.88 us
where the time goes in v1:
time: 82.2 us; the launch traced here: 81.9 us
  Pallas kernels  77.3 us (94%)
  local copies, waits for them, and re-layouts  3.88 us (5%)
    pallas_call x1, Pallas kernels, render(): pl.pallas_call(render_kernel, out_shape=(jax.ShapeDtypeStruct((groups * C...  46 us
    pallas_call x1, Pallas kernels, compose(): pl.pallas_call(compose_kernel, out_shape=jax.ShapeDtypeStruct((4, per_til...  31.3 us
    unnamed x10, local copies, waits for them, and re-layouts  3.88 us

profile of v1, /device:TPU:0, one launch (start us, length us, event | category | flops | bytes accessed | tf_op | source)
XLA Modules:
  0.0 81.9 jit_solution(3690686751846395250)
XLA Ops:
  0.7 1.3 %copy.11.target = s32[1,1,16,1]{3,2,1,0:T(8,128)} copy(s32[1,1,16,1]{2,3,1,0:T(1,128)} %param.15) | data formatting | bytes 128 | tf_op args[5]
  2.0 0.0 copy-start.2
  2.0 0.0 copy-start.3
  2.0 46.0 %render.1 = (bf16[16,2,64,128]{3,2,1,0:T(8,128)(2,1)}, s32[4,8,128]{2,1,0:T(8,128)}) custom-call(bf16[1,1,128,128,128]{4,3,2,1,0:T(8,128)(2,1)} %brick.1, f32[1,1,2]{2,1,0:T(1,128)} %shear.1, f32[1,1]{1,0:T(1,128)S(6)} %copy.13.absorb, f32[3]{0:T(128)} %color_slope.1, f32[3]{0:T(128)} %color_bias.1, s32[1,1,16]{2,1,0:T(1,128)} %rows_live.1, ...), custom_call_target="tpu_custom_call" | custom-call | flops 3221225472 | bytes 4194304 | tf_op jit(solution)/shard_map/render/pallas_call | solution.py:217
  48.0 0.0 copy-done.2
  48.0 0.0 copy-done.3
  48.0 0.0 copy-start
  48.0 1.0 %copy-done = bf16[16,2,64,128]{3,2,1,0:T(8,128)(2,1)S(1)} copy-done((bf16[16,2,64,128]{3,2,1,0:T(8,128)(2,1)S(1)}, bf16[16,2,64,128]{3,2,1,0:T(8,128)(2,1)}, u32[]{:S(2)}) %copy-start) | copy-done | bytes 524312
  49.1 0.0 copy-start.1
  49.1 0.7 copy-done.1
  49.8 31.3 %compose.1 = bf16[4,4,64,256]{3,2,1,0:T(8,128)(2,1)S(1)} custom-call(bf16[16,2,64,128]{3,2,1,0:T(8,128)(2,1)S(1)} %copy-done, s32[4,8,128]{2,1,0:T(8,128)S(1)} %copy-done.1, s32[4]{0:T(128)S(1)} %copy-done.3, s32[4]{0:T(128)S(1)} %copy-done.2), custom_call_target="tpu_custom_call" | custom-call | flops 16777216 | bytes 524288 | tf_op jit(solution)/shard_map/compose/pallas_call | solution.py:511
  81.1 0.8 copy.14
Async XLA Ops:
  2.0 46.0 %copy-start.2 = (s32[4]{0:T(128)S(1)}, s32[4]{0:T(128)}, u32[]{:S(2)}) copy-start(s32[4]{0:T(128)} %owner.3) | copy-start | bytes 52
  2.0 46.0 %copy-start.3 = (s32[4]{0:T(128)S(1)}, s32[4]{0:T(128)}, u32[]{:S(2)}) copy-start(s32[4]{0:T(128)} %view.1) | copy-start | bytes 52
  48.0 1.0 %copy-start = (bf16[16,2,64,128]{3,2,1,0:T(8,128)(2,1)S(1)}, bf16[16,2,64,128]{3,2,1,0:T(8,128)(2,1)}, u32[]{:S(2)}) copy-start(bf16[16,2,64,128]{3,2,1,0:T(8,128)(2,1)} %get-tuple-element.7.outgoing) | copy-start | bytes 1572868
  49.1 0.7 copy-start.1
